TPU v7x, 128 devices: a whole 4x4x4 slice. The times are simulated.
128 devices in a mesh: row: 32 (over z, y, core), col: 4 (over x).
Axes of the slice: x: 4, y: 4, z: 4, core: 2. Of those that a mesh axis runs over, the one named last changes fastest.
Arguments:
- cross_cov: bfloat16 [49152, 6144], P('row', 'col'), may hold values from -0.15917969 to 0.15917969
- diag_inverse: bfloat16 [2, 1536, 1536], replicated, as said below
- factor_u: bfloat16 [2, 49152, 384], P(None, 'row'), may hold values from -0.3125 to 0.3125
- factor_v: bfloat16 [2, 49152, 384], P(None, 'row'), may hold values from -0.15625 to 0.15625
- rank_ids: int32 [32, 2], P('row'), may hold values from 0 to 11
- weights_obs: float32 [3072], replicated, may hold values from -6 to 6
- observations: float32 [49152], P('row'), may hold values from -6 to 6
- prior_var: float32 [6144], P('col'), may hold values from 0.5 to 2
- incumbent: int32 [1], replicated, may hold values from 0 to 49151
- owner_perm: int32 [6144], P(('row', 'col')), may hold values from 0 to 6143, each once
Outputs:
- panel_result: bfloat16 [49152, 6144], P('row', 'col')
- variance_reduction: float32 [6144], P('col')
- improvement: float32 [6144], P(('row', 'col'))
Inputs may be any that keep to these rules, and one draw needn't show every extreme that they name: `diag_inverse`: lower triangular inverses of the factor's diagonal tiles. `owner_perm`: each prediction site once.
All inputs are finite; a program needn't handle non-finite values.
Results may differ from a plain program's by a relative error of at most 0.0064.
Values may be sent and summed in bfloat16 or wider, within the bound.
A program may use at most 192 MiB of HBM per device.

v0:
```python
import jax
import jax.numpy as jnp
from jax import lax
from jax.sharding import PartitionSpec as P


def from_root(value, axis, source):
    kept = jnp.where(lax.axis_index(axis) == source, value, 0).astype(value.dtype)
    return lax.psum(kept, axis)


def low_rank_change(left, right, xsol):
    middle = lax.dot_general(
        right, xsol, (((0,), (0,)), ((), ())), preferred_element_type=jnp.float32
    ).astype(jnp.bfloat16)
    return jnp.dot(left, middle, preferred_element_type=jnp.float32)


def shards(
    cross_cov,
    diag_inverse,
    factor_u,
    factor_v,
    rank_ids,
    weights_obs,
    observations,
    prior_var,
    incumbent,
    owner_perm,
):
    myrow = lax.axis_index("row")
    tile = cross_cov
    rmax = factor_u.shape[2]
    column_ids = jnp.arange(rmax, dtype=jnp.int32)
    solved = []
    for panel in range(2):
        local_sol = lax.cond(
            myrow == panel,
            lambda: jnp.dot(diag_inverse[panel], tile, preferred_element_type=jnp.float32).astype(
                jnp.bfloat16
            ),
            lambda: jnp.zeros_like(tile),
        )
        xsol = from_root(local_sol, "row", panel)
        solved.append(xsol)
        bucket = rank_ids[0, panel]
        left = factor_u[panel]
        right = factor_v[panel]
        masked = jnp.where(column_ids[None, :] < 32 * (bucket + 1), right, jnp.zeros_like(right))
        change = low_rank_change(left, masked, xsol)
        fresh = (tile.astype(jnp.float32) - change).astype(jnp.bfloat16)
        tile = jnp.where(myrow > panel, fresh, jnp.where(myrow == panel, xsol, tile))
    stacked = jnp.concatenate(solved, axis=0).astype(jnp.float32)
    reduction = jnp.sum(stacked * stacked, axis=0)
    mean = jnp.dot(weights_obs, stacked, precision=lax.Precision.HIGHEST)
    length = observations.shape[0]
    target = incumbent[0]
    picked = lax.dynamic_index_in_dim(observations, target % length, 0, keepdims=False)
    best = from_root(picked, "row", target // length)
    sigma = jnp.sqrt(jnp.maximum(prior_var - reduction, 0.1 * prior_var))
    zscore = (mean - best) / sigma
    density = jnp.exp(-0.5 * zscore * zscore) / jnp.sqrt(2.0 * jnp.pi)
    cumulative = 0.5 * (1.0 + lax.erf(zscore / jnp.sqrt(2.0)))
    scores = sigma * (zscore * cumulative + density)
    everyone = lax.all_gather(scores, "col", axis=0, tiled=True)
    return (tile, reduction, everyone[owner_perm])


def solution(mesh):
    placed = (
        P("row", "col"),
        P(),
        P(None, "row", None),
        P(None, "row", None),
        P("row", None),
        P(),
        P("row"),
        P("col"),
        P(),
        P(("row", "col")),
    )
    return jax.shard_map(
        shards,
        mesh=mesh,
        in_specs=placed,
        out_specs=(P("row", "col"), P("col"), P(("row", "col"))),
        check_vma=False,
    )
```

profile of v0, /device:TPU:52, one launch (start us, length us, event | category | flops | bytes accessed | tf_op | source)
XLA Modules:
  0.0 344.5 jit_solution(12792502114760791870)
XLA Ops:
  7.2 0.0 copy-start
  7.2 0.0 all-reduce.3.cloned.1.call-start
  7.2 2.5 conditional.2
  7.2 2.5 broadcast.18.clone
  9.7 2.4 broadcast_select_fusion.1
  12.2 0.0 all-reduce.3.cloned.1.call-update
  12.2 0.0 copy-start.4
  12.2 0.0 copy-start.5
  12.2 0.0 all-reduce.5.cloned.1.call-start
  12.3 6.8 %copy.25 = bf16[1536,1536]{0,1:T(8,128)(2,1)} copy(bf16[1536,1536]{1,0:T(8,128)(2,1)} %param.14) | data formatting | bytes 9437184 | tf_op args[0]
  19.0 0.0 copy-done.4
  19.0 0.6 fusion.32
  20.3 118.0 %all-reduce.3.cloned.1.call-done = bf16[1536,1536]{0,1:T(8,128)(2,1)} async-done(((bf16[1536,1536]{0,1:T(8,128)(2,1)}), bf16[1536,1536]{0,1:T(8,128)(2,1)}) %all-reduce.3.cloned.1.call-update) | async-done | bytes 4718608 | tf_op jit(solution)/shard_map/psum | solution.py:9
  138.3 0.0 copy-done.5
  138.3 14.3 %fusion.6 = bf16[1536,1536]{0,1:T(8,128)(2,1)} fusion(bf16[1536,1536]{0,1:T(8,128)(2,1)} %copy.25, bf16[1536,1536]{0,1:T(8,128)(2,1)} %all-reduce.3.cloned.1.call-done, pred[]{:T(512)S(6)} %eq.8, pred[]{:T(512)S(6)} %gt.7, bf16[2,1536,384]{2,1,0:T(8,128)(2,1)S(1)} %copy-done.5, bf16[2,1536,384]{2,1,0:T(8,128)(2,1)} %param.17, ...), kind=kOutput, calls=%fused_computation.12 | convolution fusion | flops 3636854784 | bytes 21234178 | tf_op jit(solution)/shard_map/dot_general | solution.py:16
  152.6 2.5 conditional.3
  152.6 2.5 broadcast.19.clone
  155.1 2.5 broadcast_select_fusion
  157.5 0.0 copy-start.6
  157.5 0.0 all-reduce.5.cloned.1.call-update
  158.3 1.3 dynamic_slice.4
  160.2 57.3 %psum.23 = f32[]{:T(128)} all-reduce(f32[]{:T(128)S(6)} %select_n.80), channel_id=1, replica_groups=mesh['row'=32,'col'=4] {'row'}, use_global_device_ids=true, to_apply=%region_7.8 | all-reduce | flops 1 | bytes 8 | tf_op jit(solution)/shard_map/psum | solution.py:9
  218.1 0.0 copy-done.6
  218.2 5.0 %constant_dynamic-update-slice_fusion.1 = bf16[3072,1536]{0,1:T(8,128)(2,1)} fusion(bf16[1536,1536]{0,1:T(8,128)(2,1)} %all-reduce.3.cloned.1.call-done), kind=kLoop, calls=%fused_computation.38 | loop fusion | bytes 9437184
  223.2 62.1 %all-reduce.5.cloned.1.call-done = bf16[1536,1536]{0,1:T(8,128)(2,1)} async-done(((bf16[1536,1536]{0,1:T(8,128)(2,1)}), bf16[1536,1536]{0,1:T(8,128)(2,1)}) %all-reduce.5.cloned.1.call-update) | async-done | bytes 4718608 | tf_op jit(solution)/shard_map/psum | solution.py:9
  285.3 14.4 %fusion.7 = bf16[1536,1536]{0,1:T(8,128)(2,1)} fusion(bf16[1536,1536]{0,1:T(8,128)(2,1)} %fusion.6, bf16[1536,1536]{0,1:T(8,128)(2,1)} %all-reduce.5.cloned.1.call-done, pred[]{:T(512)S(6)} %eq.16, pred[]{:T(512)S(6)} %gt.6, bf16[2,1536,384]{2,1,0:T(8,128)(2,1)S(1)} %copy-done.5, bf16[2,1536,384]{2,1,0:T(8,128)(2,1)} %param.17, ...), kind=kOutput, calls=%fused_computation.13 | convolution fusion | flops 3636854784 | bytes 21234178 | tf_op jit(solution)/shard_map/dot_general | solution.py:16
  299.7 6.6 %copy.30 = bf16[1536,1536]{1,0:T(8,128)(2,1)} copy(bf16[1536,1536]{0,1:T(8,128)(2,1)} %fusion.7) | data formatting | bytes 9437184
  306.3 4.9 %constant_dynamic-update-slice_fusion = bf16[3072,1536]{0,1:T(8,128)(2,1)} fusion(bf16[3072,1536]{0,1:T(8,128)(2,1)} %constant_dynamic-update-slice_fusion.1, bf16[1536,1536]{0,1:T(8,128)(2,1)} %all-reduce.5.cloned.1.call-done), kind=kLoop, calls=%fused_computation.37 | loop fusion | bytes 9437184 | tf_op jit(solution)/shard_map/concatenate | solution.py:53
  311.2 0.0 copy-start.1
  311.2 5.7 %multiply_reduce_fusion = f32[1536]{0:T(1024)S(1)} fusion(bf16[3072,1536]{0,1:T(8,128)(2,1)} %constant_dynamic-update-slice_fusion), kind=kLoop, calls=%fused_computation.7 | loop fusion | flops 14154240 | bytes 9443328 | tf_op jit(solution)/shard_map/reduce_sum | solution.py:54
  316.9 0.0 copy-done
  316.9 0.0 copy-start.2
  317.0 0.6 copy-done.1
  317.6 0.0 copy-start.3
  317.6 7.4 %convolution_reduce_fusion = f32[1536]{0:T(1024)S(1)} fusion(bf16[3072,1536]{0,1:T(8,128)(2,1)S(1)} %copy-done.1, f32[3072,1]{0,1:T(1,128)S(1)} %bitcast.46), kind=kOutput, calls=%fused_computation.28 | convolution fusion | flops 56623104 | bytes 9455616 | tf_op jit(solution)/shard_map/dot_general | solution.py:55
  325.0 0.0 copy-done.2
  325.0 0.0 copy-done.3
  325.0 0.6 fusion.27
  325.7 10.7 %all-gather = f32[4,1,1536]{2,1,0:T(1,128)S(1)} all-gather(f32[1,1,1536]{2,1,0:T(1,128)S(1)} %reshape.40), channel_id=1, replica_groups=mesh['row'=32,'col'=4] {'col'}, dimensions={0}, use_global_device_ids=true | all-gather | bytes 30720 | tf_op jit(solution)/shard_map/all_gather | solution.py:65
  336.4 1.3 gather_fusion
  (5 shorter events, 0.0 us)
Async XLA Ops:
  7.2 309.8 %copy-start = (f32[3072]{0:T(1024)S(1)}, f32[3072]{0:T(1024)}, u32[]{:S(2)}) copy-start(f32[3072]{0:T(1024)} %param.19) | copy-start | bytes 36868
  7.2 131.1 %all-reduce.3.cloned.1.call-start = ((), (), s32[]{:S(2)}) async-start(), calls=%async_computation | async-start | bytes 9437184 | tf_op jit(solution)/shard_map/psum | solution.py:9
  12.2 6.8 %copy-start.4 = (s32[1,2]{1,0:T(1,128)S(1)}, s32[1,2]{1,0:T(1,128)}, u32[]{:S(2)}) copy-start(s32[1,2]{1,0:T(1,128)} %param.18) | copy-start | bytes 28
  12.2 126.1 %copy-start.5 = (bf16[2,1536,384]{2,1,0:T(8,128)(2,1)S(1)}, bf16[2,1536,384]{2,1,0:T(8,128)(2,1)}, u32[]{:S(2)}) copy-start(bf16[2,1536,384]{2,1,0:T(8,128)(2,1)} %param.16) | copy-start | bytes 7077892
  12.2 273.0 %all-reduce.5.cloned.1.call-start = ((), (), s32[]{:S(2)}) async-start(), calls=%async_computation.1 | async-start | bytes 9437184 | tf_op jit(solution)/shard_map/psum | solution.py:9
  157.5 60.6 %copy-start.6 = (s32[48]{0:T(128)S(1)}, s32[48]{0:T(128)}, u32[]{:S(2)}) copy-start(s32[48]{0:T(128)} %param.23) | copy-start | bytes 580
  311.2 6.4 %copy-start.1 = (bf16[3072,1536]{0,1:T(8,128)(2,1)S(1)}, bf16[3072,1536]{0,1:T(8,128)(2,1)}, u32[]{:S(2)}) copy-start(bf16[3072,1536]{0,1:T(8,128)(2,1)} %constant_dynamic-update-slice_fusion) | copy-start | bytes 28311556
  316.9 8.0 %copy-start.2 = (f32[1536]{0:T(1024)}, f32[1536]{0:T(1024)S(1)}, u32[]{:S(2)}) copy-start(f32[1536]{0:T(1024)S(1)} %multiply_reduce_fusion) | copy-start | bytes 18436
  317.6 7.4 %copy-start.3 = (f32[1536]{0:T(1024)S(1)}, f32[1536]{0:T(1024)}, u32[]{:S(2)}) copy-start(f32[1536]{0:T(1024)} %param.21) | copy-start | bytes 18436
Sparse Core Ops, SparseCore 0:
  12.3 125.9 all-reduce.2
  157.7 127.5 all-reduce.4
where the time goes:
time: 349 us; the launch traced here: 345 us
  waiting for transfers between devices  180 us (52%)
  blocking collectives  68 us (19%)
  matrix products  36.1 us (10%)
  local copies, waits for them, and re-layouts  32 us (9%)
  between operations  16.8 us (5%)
  other arithmetic  11.3 us (3%)
    psum x2, waiting for transfers between devices, from_root(): return lax.psum(kept, axis)  180 us
    psum x1, blocking collectives, from_root(): return lax.psum(kept, axis)  57.3 us
    dot_general x2, matrix products, low_rank_change(): return jnp.dot(left, middle, preferred_element_type=jnp.float32)  28.7 us
    unnamed x18, local copies, waits for them, and re-layouts  19 us
    all_gather x1, blocking collectives, shards(): everyone = lax.all_gather(scores, 'col', axis=0, tiled=True)  10.7 us
    dot_general x1, matrix products, shards(): mean = jnp.dot(weights_obs, stacked, precision=lax.Precision.HIGHEST)  7.4 us
  transfers between devices with their start and end apart: 2, of which 2 were waited for; matrix products, arithmetic and copies ran while one was open for 4% of the time, Pallas kernels for 0%

commit v1 on v0

v1 whole, which is shorter than its diff:
```python
import jax
import jax.numpy as jnp
from jax import lax
from jax.experimental import pallas as pl
from jax.experimental.pallas import tpu as pltpu
from jax.sharding import PartitionSpec as P

MESH = pl.DeviceIdType.MESH
B = 1536
R = 384
W = 256
NB = 6
Q = 6
KS = B // Q
RC = KS // 4
NS = 2 * NB * Q
SKEW = 6
SLOTS = NS + 5 * SKEW
STAT_AT = 54
SENDS = (33825, 11, 1545, 3584, 112, 135, 1185, 480, 49200, 32805, 33825, 34080, 53248, 45060, 41985, 11520)
DEPTHS = (0, 1753, 2210, 1627, 1739, 2322, 2779, 2196, 1300, 1883, 2340, 1757, 731, 1314, 1771, 1188)
BF = jnp.bfloat16
F32 = jnp.float32


def dot(a, b):
    return jnp.dot(a, b, preferred_element_type=F32)


def lookup(index, table):
    value = jnp.int32(table[0])
    for place in range(1, len(table)):
        value = jnp.where(index == place, jnp.int32(table[place]), value)
    return value


def at0(j):
    return jnp.where(j < 3, j, 2 * j - 2)


def at1(j):
    return jnp.where(j < 3, 2 * j + 3, j + 6)


def solve_kernel(
    cov, dinv, fu, fv, rank, wobs, obs, pvar, inc,
    res, stat,
    xs, ub, vb, vt, db, mb, acc, wv, ov, pv, st, red, mean, bs, rk, ic,
    load, chunk_in, slab_in, tree_out, slab_out, best_in, best_out, stat_in, stat_out, plane_in, plane_out,
):
    myrow = lax.axis_index("row")
    x = lax.axis_index("col")
    z = myrow // 8
    y = (myrow // 2) % 4
    c = myrow % 2
    node = z * 4 + y
    source = node == 0

    def rid(zz, yy, cc):
        return ((zz + 4) % 4) * 8 + ((yy + 4) % 4) * 2 + cc

    around = [rid(z, y + 1, 0), rid(z + 1, y, 0), rid(z, y - 1, 0), rid(z - 1, y, 0)]
    sibling = rid(z, y, 1 - c)
    sends = lookup(node, SENDS)
    depths = lookup(node, DEPTHS)

    barrier = pltpu.get_barrier_semaphore()

    def hello(row, col):
        pl.semaphore_signal(barrier, inc=1, device_id=(row, col), device_id_type=MESH)

    hello(sibling, x)

    @pl.when(c == 0)
    def _():
        for other in around + [rid(z, y + 2, 0), rid(z + 2, y, 0)]:
            hello(other, x)

    @pl.when(jnp.logical_and(c == 1, source))
    def _():
        for dx in range(1, 4):
            hello(myrow, (x + dx) % 4)

    def local(src, dst, place):
        return pltpu.make_async_copy(src, dst, load.at[place])

    def load_cov():
        return local(cov, res, 0)

    def load_d():
        return local(dinv.at[c], db, 1)

    def load_u(p):
        return local(fu.at[p], ub.at[:, pl.ds(p * R, R)], 2 + p)

    def load_v(p):
        return local(fv.at[p], vb.at[p], 4 + p)

    def load_rank():
        return local(rank, rk, 6)

    def load_inc():
        return local(inc, ic, 7)

    def load_obs():
        return local(obs, ov, 8)

    def load_w():
        return local(wobs, wv, 9)

    def load_pv():
        return local(pvar, pv, 10)

    @pl.when(source)
    def _():
        load_cov().start()
        load_d().start()

    load_inc().start()
    load_obs().start()
    load_rank().start()
    for p in range(2):
        load_v(p).start()

    @pl.when(jnp.logical_not(source))
    def _():
        load_cov().start()

    for p in range(2):
        load_u(p).start()
    load_w().start()
    load_pv().start()

    def triangular(k, j):
        cols = pl.ds(pl.multiple_of(j * W, W), W)
        for r in range(B // 256):
            deep = (r + 1) * 256
            xs[k, pl.ds(r * 256, 256), :] = dot(db[pl.ds(r * 256, 256), pl.ds(0, deep)], res[pl.ds(0, deep), cols]).astype(BF)
        res[:, cols] = xs[k]

    def block_copy(k, place):
        return pltpu.make_async_remote_copy(
            xs.at[k], xs.at[k], slab_out.at[place], slab_in.at[k * Q], device_id=(sibling, x), device_id_type=MESH
        )

    def slab_copy(m):
        part = xs.at[m // Q, pl.ds(pl.multiple_of((m % Q) * KS, KS), KS)]
        return pltpu.make_async_remote_copy(
            part, part, slab_out.at[0], slab_in.at[m], device_id=(sibling, x), device_id_type=MESH
        )

    def chunk_copy(i, t, d):
        part = xs.at[i // Q, pl.ds(pl.multiple_of((i % Q) * KS + t * RC, RC), RC)]
        return pltpu.make_async_remote_copy(
            part, part, tree_out.at[t, d], chunk_in.at[i, t], device_id=(around[d], x), device_id_type=MESH
        )

    def drain(sem, blocks):
        part = xs.at[pl.ds(0, blocks)]
        pltpu.make_async_remote_copy(
            part, part, sem, slab_in.at[0], device_id=(sibling, x), device_id_type=MESH
        ).wait_send()

    def best_copy(place, slot, row):
        return pltpu.make_async_remote_copy(
            bs.at[0], bs.at[slot], best_out.at[place], best_in.at[slot], device_id=(row, x), device_id_type=MESH
        )

    def stat_copy(place, row):
        return pltpu.make_async_remote_copy(
            st, st, stat_out.at[place], stat_in, device_id=(row, x), device_id_type=MESH
        )

    @pl.when(jnp.logical_and(source, c == 0))
    def _():
        load_cov().wait()
        load_d().wait()
        triangular(0, 0)

    for p in range(2):
        load_v(p).wait()

    @pl.when(myrow > 0)
    def _():
        for p in range(2):
            for q in range(Q):
                vt[p, q] = vb[p, pl.ds(q * KS, KS), :].T

    load_rank().wait()

    def masked(value, p):
        ids = lax.broadcasted_iota(jnp.int32, value.shape, 0)
        return jnp.where(ids < 32 * (rk[0, p] + 1), value, 0.0).astype(BF)

    @pl.when(c == 0)
    def _():
        pl.semaphore_wait(barrier, 7)

    @pl.when(jnp.logical_and(c == 1, source))
    def _():
        pl.semaphore_wait(barrier, 4)

    @pl.when(jnp.logical_and(c == 1, jnp.logical_not(source)))
    def _():
        pl.semaphore_wait(barrier, 1)

    load_inc().wait()
    load_obs().wait()
    spots = myrow * B + lax.broadcasted_iota(jnp.int32, (12, 128), 0) * 128 + lax.broadcasted_iota(jnp.int32, (12, 128), 1)
    mine = jnp.sum(jnp.where(spots == ic[0], ov[...], 0.0), axis=0, keepdims=True)
    bs[0] = jnp.where(lax.broadcasted_iota(jnp.int32, (8, 128), 0) == 0, mine, 0.0)

    @pl.when(c == 1)
    def _():
        best_copy(0, 1, sibling).start()

    def best_from_sibling():
        best_copy(0, 1, sibling).wait_recv()
        bs[0] = bs[0] + bs[1]

        @pl.when(z > 0)
        def _():
            best_copy(1, 1 + z, rid(0, y, 0)).start()

    def best_over_z():
        for slot in (2, 3, 4):
            best_copy(1, slot, sibling).wait_recv()
        bs[0] = bs[0] + (bs[2] + bs[3] + bs[4])

        @pl.when(y > 0)
        def _():
            best_copy(1, 4 + y, rid(0, 0, 0)).start()

    def best_over_y():
        for slot in (5, 6, 7):
            best_copy(1, slot, sibling).wait_recv()
        bs[0] = bs[0] + (bs[5] + bs[6] + bs[7])
        best_copy(1, 2, sibling).start()

    @pl.when(jnp.logical_and(source, c == 0))
    def _():
        block_copy(0, 0).start()

        def slot(s, carry):
            k = s // Q
            second = jnp.logical_or(k >= 9, jnp.logical_and(k >= 3, k % 2 == 1))

            @pl.when(jnp.logical_and(second, s % Q == 0))
            def _():
                block_copy(k, 0).wait_recv()

            for t in range(4):
                chunk_copy(s, t, t).start()

            @pl.when(jnp.logical_and(s % 2 == 0, s < 10))
            def _():
                j = s // 2 + 1
                triangular(at0(j), j)
                block_copy(at0(j), 0).start()

            @pl.when(s == 10)
            def _():
                best_from_sibling()

            @pl.when(s == 12)
            def _():
                best_over_z()

            @pl.when(s == 14)
            def _():
                best_over_y()

            @pl.when(s == STAT_AT)
            def _():
                stat_copy(0, sibling).wait_recv()
                stat_copy(0, around[0]).start()

            return carry

        lax.fori_loop(0, NS, slot, 0)
        stat_copy(0, sibling).wait_send()
        best_copy(1, 2, sibling).wait_send()
        for t in range(4):
            drain(tree_out.at[t, t], NB // 2)
        drain(slab_out.at[0], NB)
        for p in range(2):
            load_u(p).wait()
        load_w().wait()
        load_pv().wait()

    @pl.when(jnp.logical_and(source, c == 1))
    def _():
        load_cov().wait()
        load_d().wait()
        for p in range(2):
            load_u(p).wait()
        load_w().wait()
        load_pv().wait()
        terms = []
        for p in range(2):
            row = jnp.concatenate([wv[pl.ds(12 * p + g, 1), :] for g in range(12)], axis=1)
            high = row.astype(BF)
            rest = row - high.astype(F32)
            middle = rest.astype(BF)
            low = (rest - middle.astype(F32)).astype(BF)
            ids = lax.broadcasted_iota(jnp.int32, (16, B), 0)
            terms.append(
                jnp.where(
                    ids == 0, high.astype(F32),
                    jnp.where(ids == 1, middle.astype(F32), jnp.where(ids == 2, low.astype(F32), 0.0)),
                ).astype(BF)
            )

        def block(j, carry):
            first, second = at0(j), at1(j)
            cols = pl.ds(pl.multiple_of(j * W, W), W)
            block_copy(first, 0).wait_recv()
            m = dot(vt[0, 0], xs[first, pl.ds(0, KS), :])
            for q in range(1, Q):
                m += dot(vt[0, q], xs[first, pl.ds(q * KS, KS), :])
            mb[0, pl.ds(0, R), :] = masked(m, 0)
            for r in range(B // 256):
                rows = pl.ds(r * 256, 256)
                res[rows, cols] = (res[rows, cols].astype(F32) - dot(ub[rows, pl.ds(0, R)], mb[0, pl.ds(0, R), :])).astype(BF)
            triangular(second, j)
            block_copy(second, 0).start()
            squares = jnp.zeros((8, W), F32)
            total = jnp.zeros((16, W), F32)
            for p, k in ((0, first), (1, second)):
                total += dot(terms[p], xs[k])
                for r in range(B // 256):
                    part = xs[k, pl.ds(r * 256, 256), :].astype(F32)
                    squares += jnp.sum((part * part).reshape(32, 8, W), axis=0)
            line = jnp.sum(squares, axis=0, keepdims=True)
            mline = jnp.sum(total, axis=0, keepdims=True)
            for half in range(2):
                red[pl.ds(2 * j + half, 1), :] = line[:, half * 128 : (half + 1) * 128]
                mean[pl.ds(2 * j + half, 1), :] = mline[:, half * 128 : (half + 1) * 128]
            return carry

        lax.fori_loop(0, NB, block, 0)
        best_copy(1, 2, sibling).wait_recv()
        best = jnp.sum(bs[2])
        prior = pv[...]
        reduction = red[pl.ds(0, 12), :]
        sigma = jnp.sqrt(jnp.maximum(prior - reduction, 0.1 * prior))
        zscore = (mean[pl.ds(0, 12), :] - best) / sigma
        density = jnp.exp(-0.5 * zscore * zscore) / jnp.sqrt(jnp.float32(2.0 * jnp.pi))
        cumulative = 0.5 * (1.0 + lax.erf(zscore / jnp.sqrt(jnp.float32(2.0))))
        st[4, pl.ds(0, 12), :] = reduction
        st[x, pl.ds(0, 12), :] = sigma * (zscore * cumulative + density)

        def plane_copy(dx):
            return pltpu.make_async_remote_copy(
                st.at[x], st.at[x], plane_out.at[dx], plane_in.at[x], device_id=(myrow, (x + dx) % 4), device_id_type=MESH
            )

        for dx in range(1, 4):
            plane_copy(dx).start()
        for dx in range(1, 4):
            other = (x + dx) % 4
            pltpu.make_async_remote_copy(
                st.at[other], st.at[other], plane_out.at[dx], plane_in.at[other],
                device_id=(myrow, other), device_id_type=MESH,
            ).wait_recv()
        stat_copy(0, sibling).start()
        for dx in range(1, 4):
            plane_copy(dx).wait_send()
        stat_copy(0, sibling).wait_send()
        drain(slab_out.at[0], NB)

    @pl.when(jnp.logical_not(source))
    def _():
        longest = jnp.int32(0)
        for t in range(4):
            longest = jnp.maximum(longest, (depths // 8**t) % 8)

        @pl.when(c == 0)
        def _():
            best_from_sibling()

        def sends_on(t, d):
            return (sends // 2 ** (4 * t + d)) % 2 == 1

        load_cov().wait()
        for p in range(2):
            load_u(p).wait()
        load_w().wait()
        load_pv().wait()

        def update(j, first, count):
            rows = pl.ds(pl.multiple_of(first, KS), count)
            cols = pl.ds(pl.multiple_of(j * W, W), W)
            res[rows, cols] = (res[rows, cols].astype(F32) - dot(ub[rows, :], mb[j])).astype(BF)

        def slot(s, carry):
            @pl.when(c == 0)
            def _():
                for t in range(4):
                    i = s - SKEW * ((depths // 8**t) % 8)

                    @pl.when(jnp.logical_and(i >= 0, i < NS))
                    def _():
                        chunk_copy(i, t, 0).wait_recv()
                        for d in range(4):
                            @pl.when(sends_on(t, d))
                            def _():
                                chunk_copy(i, t, d).start()

                    if t == 0:
                        @pl.when(i == STAT_AT)
                        def _():
                            stat_copy(0, sibling).wait_recv()
                            for d in range(4):
                                @pl.when(sends_on(0, d))
                                def _():
                                    stat_copy(d, around[d]).start()
                            stat_copy(4, sibling).start()

            @pl.when(jnp.logical_and(s == 6, jnp.logical_and(c == 0, z == 0)))
            def _():
                best_over_z()

            m = s - SKEW * longest

            @pl.when(jnp.logical_and(m >= 0, m < NS))
            def _():
                @pl.when(c == 0)
                def _():
                    slab_copy(m).start()

                @pl.when(c == 1)
                def _():
                    slab_copy(m).wait_recv()

                k = m // Q
                q = m % Q
                second = jnp.logical_or(k >= 9, jnp.logical_and(k >= 3, k % 2 == 1))
                p = second.astype(jnp.int32)
                j = jnp.where(second, jnp.where(k >= 9, k - 6, (k - 3) // 2), jnp.where(k < 3, k, (k + 2) // 2))
                part = dot(vt[p, q], xs[k, pl.ds(pl.multiple_of(q * KS, KS), KS), :])

                @pl.when(q == 0)
                def _():
                    acc[...] = part

                @pl.when(jnp.logical_and(q > 0, q < Q - 1))
                def _():
                    acc[...] = acc[...] + part

                @pl.when(q == Q - 1)
                def _():
                    mb[j, pl.ds(pl.multiple_of(p * R, R), R), :] = masked(acc[...] + part, p)

                before = k - 1
                was = jnp.logical_or(before >= 9, jnp.logical_and(before >= 3, before % 2 == 1))

                @pl.when(was)
                def _():
                    update(jnp.where(before >= 9, before - 6, (before - 3) // 2), q * KS, KS)

            return carry

        lax.fori_loop(0, SLOTS, slot, 0)

        def last(q, carry):
            update(NB - 1, q * KS, KS)
            return carry

        lax.fori_loop(0, Q, last, 0)

        @pl.when(c == 0)
        def _():
            drain(slab_out.at[0], 2 * NB)
            stat_copy(4, sibling).wait_send()
            for d in range(4):
                @pl.when(sends_on(0, d))
                def _():
                    stat_copy(d, around[d]).wait_send()
                for t in range(4):
                    @pl.when(sends_on(t, d))
                    def _():
                        drain(tree_out.at[t, d], NB // 2)

            @pl.when(jnp.logical_or(z > 0, y > 0))
            def _():
                best_copy(1, 2, sibling).wait_send()

        @pl.when(c == 1)
        def _():
            stat_copy(0, sibling).wait_recv()

    @pl.when(c == 1)
    def _():
        best_copy(0, 1, sibling).wait_send()

    stat[...] = st[...]


def place_kernel(res, stat, perm, out, var, imp, lines, slots, sems):
    whole = pltpu.make_async_copy(res, out, sems.at[0])
    whole.start()
    scores = pltpu.make_async_copy(stat, lines, sems.at[1])
    scores.start()
    owners = pltpu.make_async_copy(perm, slots, sems.at[2])
    owners.start()
    var[...] = stat[4, pl.ds(0, 12), :]
    scores.wait()
    owners.wait()

    def pick(i, carry):
        site = slots[i]
        imp[i] = lines[site // B, (site % B) // 128, site % 128]
        return carry

    lax.fori_loop(0, imp.shape[0], pick, 0)
    whole.wait()


def shards(cross_cov, diag_inverse, factor_u, factor_v, rank_ids, weights_obs, observations, prior_var, incumbent, owner_perm):
    hbm = pl.BlockSpec(memory_space=pl.ANY)
    vmem = pl.BlockSpec(memory_space=pltpu.VMEM)
    dma = pltpu.SemaphoreType.DMA
    solved, stats = pl.pallas_call(
        solve_kernel,
        name="solve",
        out_shape=(pltpu.VMEM((B, B), BF), pltpu.VMEM((5, 16, 128), F32)),
        in_specs=[hbm] * 9,
        out_specs=(vmem, vmem),
        scratch_shapes=[
            pltpu.VMEM((2 * NB, B, W), BF),
            pltpu.VMEM((B, 2 * R), BF),
            pltpu.VMEM((2, B, R), BF),
            pltpu.VMEM((2, Q, R, KS), BF),
            pltpu.VMEM((B, B), BF),
            pltpu.VMEM((NB, 2 * R, W), BF),
            pltpu.VMEM((R, W), F32),
            pltpu.VMEM((24, 128), F32),
            pltpu.VMEM((12, 128), F32),
            pltpu.VMEM((12, 128), F32),
            pltpu.VMEM((5, 16, 128), F32),
            pltpu.VMEM((16, 128), F32),
            pltpu.VMEM((16, 128), F32),
            pltpu.VMEM((8, 8, 128), F32),
            pltpu.SMEM((1, 2), jnp.int32),
            pltpu.SMEM((1,), jnp.int32),
            dma((11,)),
            dma((NS, 4)),
            dma((NS,)),
            dma((4, 4)),
            dma((1,)),
            dma((8,)),
            dma((2,)),
            dma,
            dma((5,)),
            dma((4,)),
            dma((4,)),
        ],
        compiler_params=pltpu.CompilerParams(collective_id=0, has_side_effects=True, vmem_limit_bytes=48 << 20),
        cost_estimate=pl.CostEstimate(flops=7_250_000_000, bytes_accessed=9_400_000, transcendentals=0),
    )(
        cross_cov, diag_inverse, factor_u, factor_v, rank_ids, weights_obs.reshape(24, 128),
        observations.reshape(12, 128), prior_var.reshape(12, 128), incumbent,
    )
    slots = owner_perm.shape[0]
    result, reduction, improvement = pl.pallas_call(
        place_kernel,
        name="place",
        out_shape=(
            jax.ShapeDtypeStruct((B, B), BF),
            jax.ShapeDtypeStruct((12, 128), F32),
            jax.ShapeDtypeStruct((slots,), F32),
        ),
        in_specs=[vmem, vmem, hbm],
        out_specs=(hbm, vmem, pl.BlockSpec(memory_space=pltpu.SMEM)),
        scratch_shapes=[pltpu.SMEM((5, 16, 128), F32), pltpu.SMEM((slots,), jnp.int32), dma((3,))],
        compiler_params=pltpu.CompilerParams(vmem_limit_bytes=16 << 20),
    )(solved, stats, owner_perm)
    return result, reduction.reshape(B), improvement


def solution(mesh):
    placed = (
        P("row", "col"), P(), P(None, "row", None), P(None, "row", None), P("row", None),
        P(), P("row"), P("col"), P(), P(("row", "col")),
    )
    return jax.shard_map(
        shards, mesh=mesh, in_specs=placed, out_specs=(P("row", "col"), P("col"), P(("row", "col"))), check_vma=False
    )
```

time: 349 us -> 80.6 us (0.23)
  the two profiles are of different devices: /device:TPU:52 before, /device:TPU:53 now
where the time goes in v1:
time: 80.6 us; the launch traced here: 80.3 us
  Pallas kernels  76.2 us (95%)
  local copies, waits for them, and re-layouts  2.75 us (3%)
  between operations  1.31 us (2%)
    pallas_call x1, Pallas kernels, shards(): pl.pallas_call(solve_kernel, name='solve', out_shape=(pltpu.VMEM((B, B),...  73.2 us
    pallas_call x1, Pallas kernels, shards(): pl.pallas_call(place_kernel, name='place', out_shape=(jax.ShapeDtypeStruc...  2.99 us
    unnamed x10, local copies, waits for them, and re-layouts  2.75 us

profile of v1, /device:TPU:53, one launch (start us, length us, event | category | flops | bytes accessed | tf_op | source)
XLA Modules:
  0.0 80.3 jit_solution(9352295392084577843)
XLA Ops:
  1.3 0.0 copy-start.1
  1.3 0.7 copy-done.1
  2.0 0.0 copy-start.2
  2.0 0.7 copy-done.2
  2.7 0.0 copy-start.3
  2.7 0.7 copy-done.3
  3.4 0.0 copy-start.4
  3.4 0.7 copy-done.4
  4.0 0.0 copy-start
  4.0 73.2 %solve.1 = (bf16[1536,1536]{1,0:T(8,128)(2,1)S(1)}, f32[5,16,128]{2,1,0:T(8,128)S(1)}) custom-call(bf16[1536,1536]{1,0:T(8,128)(2,1)} %cov.1, bf16[2,1536,1536]{2,1,0:T(8,128)(2,1)} %dinv.1, bf16[2,1536,384]{2,1,0:T(8,128)(2,1)} %fu.1, bf16[2,1536,384]{2,1,0:T(8,128)(2,1)} %fv.1, s32[1,2]{1,0:T(1,128)S(1)} %copy-done.4, f32[24,128]{1,0:T(8,128)S(1)} %bitcast.4, ...), custom_call_target="tpu_custom_call" | custom-call | flops 7249999872 | bytes 9400000 | tf_op jit(solution)/shard_map/solve/pallas_call | solution.py:524
  77.3 0.0 copy-done
  77.3 3.0 %place.1 = (bf16[1536,1536]{1,0:T(8,128)(2,1)}, f32[12,128]{1,0:T(8,128)}, f32[48]{0:T(128)}) custom-call(bf16[1536,1536]{1,0:T(8,128)(2,1)S(1)} %get-tuple-element.8.res, f32[5,16,128]{2,1,0:T(8,128)S(1)} %get-tuple-element.9.stat, s32[48]{0:T(128)S(1)} %copy-done), custom_call_target="tpu_custom_call" | custom-call | tf_op jit(solution)/shard_map/place/pallas_call | solution.py:566
Async XLA Ops:
  1.3 0.7 copy-start.1
  2.0 0.7 copy-start.2
  2.7 0.7 copy-start.3
  3.4 0.7 copy-start.4
  4.0 73.2 %copy-start = (s32[48]{0:T(128)S(1)}, s32[48]{0:T(128)}, u32[]{:S(2)}) copy-start(s32[48]{0:T(128)} %perm.1) | copy-start | bytes 580

commit v2 on v1

v2 whole, which is shorter than its diff:
```python
import functools
import jax
import jax.numpy as jnp
from jax import lax
from jax.experimental import pallas as pl
from jax.experimental.pallas import tpu as pltpu
from jax.sharding import PartitionSpec as P

MESH = pl.DeviceIdType.MESH
B = 1536
R = 384
W = 256
NB = 6
Q = 2
KS = B // Q
RC = KS // 4
NS = 2 * NB * Q
AHEAD = 6
STAT_AT = NS - 1
UPDATE_AT = {2: (0, 1), 3: (1, 2), 4: (1, 3), 6: (2, 4)}[Q]
PLACES = (0, 0, 4, 2, 1, 8, 12, 9, 5, 15, 16, 13, 3, 11, 14, 10)
ROLES = (
    ((1, (0, 1, 3)), (3, ()), (3, ()), (3, ())),
    ((2, (0, 3)), (4, ()), (2, (1, 2)), (4, ())),
    ((2, (0, 1, 2)), (2, (3,)), (4, ()), (4, ())),
    ((3, (0,)), (3, (1, 3)), (3, (2,)), (5, ())),
    ((4, (0,)), (4, (1,)), (4, (2,)), (4, (3,))),
)
EARLY = tuple(AHEAD if any(not children for _, children in role) else 0 for role in ROLES)
LEADS = tuple(EARLY[place // 4] if ROLES[place // 4][-place % 4][1] else 0 for place in PLACES)
FIRST = tuple(sum(1 << (d + place) % 4 for d in ROLES[place // 4][-place % 4][1]) for place in PLACES)
BF = jnp.bfloat16
F32 = jnp.float32


def dot(a, b):
    return jnp.dot(a, b, preferred_element_type=F32)


def lookup(index, table):
    value = jnp.int32(table[0])
    for place in range(1, len(table)):
        value = jnp.where(index == place, jnp.int32(table[place]), value)
    return value


def pick(index, values):
    value = values[0]
    for place in range(1, len(values)):
        value = jnp.where(index == place, values[place], value)
    return value


def at0(j):
    return j


def at1(j):
    return NB + j


def solve_kernel(
    cov, dinv, fu, fv, rank, wobs, obs, pvar, inc,
    res, stat,
    xs, ub, vb, vt, db, mb, acc, wv, ov, pv, st, own, theirs, bs, rk, ic,
    load, chunk_in, slab_in, tree_out, slab_out, best_in, best_out, stat_in, stat_out, plane_in, plane_out,
):
    myrow = lax.axis_index("row")
    x = lax.axis_index("col")
    z = myrow // 8
    y = (myrow // 2) % 4
    c = myrow % 2
    node = z * 4 + y
    source = node == 0

    def rid(zz, yy, cc):
        return ((zz + 4) % 4) * 8 + ((yy + 4) % 4) * 2 + cc

    hub = (c == 0) == source

    def hub_of(zz, yy):
        first = jnp.logical_and((zz + 4) % 4 == 0, (yy + 4) % 4 == 0)
        return rid(zz, yy, jnp.where(first, 0, 1))

    around = [hub_of(z, y + 1), hub_of(z + 1, y), hub_of(z, y - 1), hub_of(z - 1, y)]
    sibling = rid(z, y, 1 - c)
    place = lookup(node, PLACES)
    role = place // 4
    turns = place % 4

    barrier = pltpu.get_barrier_semaphore()

    def hello(row, col):
        pl.semaphore_signal(barrier, inc=1, device_id=(row, col), device_id_type=MESH)

    hello(sibling, x)

    @pl.when(hub)
    def _():
        for other in around + [hub_of(z, y + 2), hub_of(z + 2, y)]:
            hello(other, x)

    @pl.when(jnp.logical_and(c == 1, source))
    def _():
        for dx in range(1, 4):
            hello(myrow, (x + dx) % 4)

    def local(src, dst, place):
        return pltpu.make_async_copy(src, dst, load.at[place])

    def load_cov():
        return local(cov, res, 0)

    def load_cov_block(j):
        cols = pl.ds(j * W, W)
        return local(cov.at[:, cols], res.at[:, cols], 11 + j)

    def load_d(r):
        part = (pl.ds(r * W, W), pl.ds(0, (r + 1) * W))
        return local(dinv.at[(c, *part)], db.at[part], 17 + r)

    def load_u(p):
        return local(fu.at[p], ub.at[:, pl.ds(p * R, R)], 2 + p)

    def load_v(p):
        return local(fv.at[p], vb.at[p], 4 + p)

    def load_rank():
        return local(rank, rk, 6)

    def load_inc():
        return local(inc, ic, 7)

    def load_obs():
        return local(obs, ov, 8)

    def load_w():
        return local(wobs, wv, 9)

    def load_pv():
        return local(pvar, pv, 10)

    @pl.when(source)
    def _():
        load_cov_block(0).start()
        for r in range(NB):
            load_d(r).start()

    load_inc().start()
    load_obs().start()

    @pl.when(myrow > 0)
    def _():
        load_rank().start()
        for p in range(2):
            load_v(p).start()

    @pl.when(source)
    def _():
        for j in range(1, NB):
            load_cov_block(j).start()

    @pl.when(jnp.logical_not(source))
    def _():
        load_cov().start()

    @pl.when(myrow > 0)
    def _():
        for p in range(2):
            load_u(p).start()

    @pl.when(source)
    def _():
        load_w().start()

    @pl.when(myrow == 1)
    def _():
        load_pv().start()

    def block_rows(k, first=0, count=B):
        return pl.ds(pl.multiple_of(k * B + first, 128), count)

    def triangular(k, j):
        cols = pl.ds(pl.multiple_of(j * W, W), W)
        for r in range(NB):
            deep = (r + 1) * W
            xs[block_rows(k, r * W, W), :] = dot(db[pl.ds(r * W, W), pl.ds(0, deep)], res[pl.ds(0, deep), cols]).astype(BF)
        res[:, cols] = xs[block_rows(k), :]

    def block_copy(k, place):
        part = xs.at[block_rows(k)]
        return pltpu.make_async_remote_copy(
            part, part, slab_out.at[place], slab_in.at[k * Q], device_id=(sibling, x), device_id_type=MESH
        )

    def slab_copy(m):
        part = xs.at[pl.ds(pl.multiple_of(m * KS, KS), KS)]
        return pltpu.make_async_remote_copy(
            part, part, slab_out.at[0], slab_in.at[m], device_id=(sibling, x), device_id_type=MESH
        )

    def chunk_copy(i, t, d):
        part = xs.at[pl.ds(pl.multiple_of(i * KS + t * RC, RC), RC)]
        return pltpu.make_async_remote_copy(
            part, part, tree_out.at[t, d], chunk_in.at[i * 4 + t], device_id=(around[d], x), device_id_type=MESH
        )

    def drain(sem, blocks):
        part = xs.at[pl.ds(0, blocks * B)]
        pltpu.make_async_remote_copy(
            part, part, sem, slab_in.at[0], device_id=(sibling, x), device_id_type=MESH
        ).wait_send()

    def best_copy(place, slot, row):
        return pltpu.make_async_remote_copy(
            bs.at[0], bs.at[slot], best_out.at[place], best_in.at[slot], device_id=(row, x), device_id_type=MESH
        )

    def stat_copy(place, row):
        return pltpu.make_async_remote_copy(
            st, st, stat_out.at[place], stat_in, device_id=(row, x), device_id_type=MESH
        )

    @pl.when(source)
    def _():
        load_cov_block(0).wait()
        for r in range(NB):
            load_d(r).wait()

    @pl.when(myrow == 0)
    def _():
        triangular(0, 0)

    @pl.when(myrow > 0)
    def _():
        for p in range(2):
            load_v(p).wait()
            vt[p] = vb[p].T
        load_rank().wait()

    def masked(value, p):
        ids = lax.broadcasted_iota(jnp.int32, value.shape, 0)
        return jnp.where(ids < 32 * (rk[0, p] + 1), value, 0.0).astype(BF)

    @pl.when(hub)
    def _():
        pl.semaphore_wait(barrier, 7)

    @pl.when(jnp.logical_and(c == 1, source))
    def _():
        pl.semaphore_wait(barrier, 4)

    @pl.when(jnp.logical_and(c == 0, jnp.logical_not(source)))
    def _():
        pl.semaphore_wait(barrier, 1)

    load_inc().wait()
    load_obs().wait()
    spots = myrow * B + lax.broadcasted_iota(jnp.int32, (12, 128), 0) * 128 + lax.broadcasted_iota(jnp.int32, (12, 128), 1)
    mine = jnp.sum(jnp.where(spots == ic[0], ov[...], 0.0), axis=0, keepdims=True)
    bs[0] = jnp.where(lax.broadcasted_iota(jnp.int32, (8, 128), 0) == 0, mine, 0.0)

    @pl.when(jnp.logical_not(hub))
    def _():
        best_copy(0, 1, sibling).start()

    def best_from_sibling():
        best_copy(0, 1, sibling).wait_recv()
        bs[0] = bs[0] + bs[1]

        @pl.when(z > 0)
        def _():
            best_copy(1, 1 + z, hub_of(0, y)).start()

    def best_over_z():
        for slot in (2, 3, 4):
            best_copy(1, slot, sibling).wait_recv()
        bs[0] = bs[0] + (bs[2] + bs[3] + bs[4])

        @pl.when(y > 0)
        def _():
            best_copy(1, 4 + y, hub_of(0, 0)).start()

    def best_over_y():
        for slot in (5, 6, 7):
            best_copy(1, slot, sibling).wait_recv()
        bs[0] = bs[0] + (bs[5] + bs[6] + bs[7])
        best_copy(1, 2, sibling).start()

    def weights(p):
        row = jnp.concatenate([wv[pl.ds(12 * p + g, 1), :] for g in range(12)], axis=1)
        high = row.astype(BF).astype(F32)
        middle = (row - high).astype(BF).astype(F32)
        low = row - high - middle
        ids = lax.broadcasted_iota(jnp.int32, (16, B), 0)
        return jnp.where(ids == 0, high, jnp.where(ids == 1, middle, jnp.where(ids == 2, low, 0.0))).astype(BF)

    def tally(k, j, terms):
        squares = jnp.zeros((8, W), F32)
        for r in range(NB):
            part = xs[block_rows(k, r * W, W), :].astype(F32)
            squares += jnp.sum((part * part).reshape(W // 8, 8, W), axis=0)
        line = jnp.sum(squares, axis=0, keepdims=True)
        mline = jnp.sum(dot(terms, xs[block_rows(k), :]), axis=0, keepdims=True)
        for half in range(2):
            own[0, pl.ds(2 * j + half, 1), :] = line[:, half * 128 : (half + 1) * 128]
            own[1, pl.ds(2 * j + half, 1), :] = mline[:, half * 128 : (half + 1) * 128]

    def sums_copy():
        return pltpu.make_async_remote_copy(
            own, theirs, best_out.at[2], best_in.at[0], device_id=(sibling, x), device_id_type=MESH
        )

    @pl.when(jnp.logical_and(source, c == 0))
    def _():
        block_copy(0, 0).start()
        for j in range(1, NB):
            load_cov_block(j).wait()
        load_w().wait()
        terms = weights(0)

        def slot(s, carry):
            k = s // Q

            @pl.when(jnp.logical_and(k >= NB, s % Q == 0))
            def _():
                block_copy(k, 0).wait_recv()

            for t in range(4):
                chunk_copy(s, t, t).start()

            @pl.when(jnp.logical_and(s % 2 == 0, s < 10))
            def _():
                j = s // 2 + 1
                triangular(at0(j), j)
                block_copy(at0(j), 0).start()

            @pl.when(s == 6 * Q)
            def _():
                best_from_sibling()

            @pl.when(s == 6 * Q + 1)
            def _():
                best_over_z()

            @pl.when(s == 7 * Q)
            def _():
                best_over_y()

            after = s - 4 * Q

            @pl.when(jnp.logical_and(jnp.logical_and(after >= 0, after < 12), after % 2 == 0))
            def _():
                tally(at0(after // 2), after // 2, terms)

            @pl.when(after == 11)
            def _():
                sums_copy().start()

            @pl.when(s == STAT_AT)
            def _():
                stat_copy(0, sibling).wait_recv()
                stat_copy(0, around[0]).start()

            return carry

        lax.fori_loop(0, NS, slot, 0)
        sums_copy().wait_send()
        stat_copy(0, sibling).wait_send()
        best_copy(1, 2, sibling).wait_send()
        for t in range(4):
            drain(tree_out.at[t, t], NB // 2)
        drain(slab_out.at[0], NB)

    @pl.when(jnp.logical_and(source, c == 1))
    def _():
        for j in range(1, NB):
            load_cov_block(j).wait()
        for p in range(2):
            load_u(p).wait()
        load_w().wait()
        load_pv().wait()
        terms = weights(1)

        def block(j, carry):
            first, second = at0(j), at1(j)
            cols = pl.ds(pl.multiple_of(j * W, W), W)
            block_copy(first, 0).wait_recv()
            mb[0, pl.ds(0, R), :] = masked(dot(vt[0], xs[block_rows(first), :]), 0)
            res[:, cols] = (res[:, cols].astype(F32) - dot(ub[:, pl.ds(0, R)], mb[0, pl.ds(0, R), :])).astype(BF)
            triangular(second, j)
            block_copy(second, 0).start()
            tally(second, j, terms)
            return carry

        lax.fori_loop(0, NB, block, 0)
        best_copy(1, 2, sibling).wait_recv()
        best = jnp.sum(bs[2])
        prior = pv[...]
        sums_copy().wait_recv()
        reduction = own[0, pl.ds(0, 12), :] + theirs[0, pl.ds(0, 12), :]
        mean = own[1, pl.ds(0, 12), :] + theirs[1, pl.ds(0, 12), :]
        sigma = jnp.sqrt(jnp.maximum(prior - reduction, 0.1 * prior))
        zscore = (mean - best) / sigma
        density = jnp.exp(-0.5 * zscore * zscore) / jnp.sqrt(jnp.float32(2.0 * jnp.pi))
        cumulative = 0.5 * (1.0 + lax.erf(zscore / jnp.sqrt(jnp.float32(2.0))))
        st[4, pl.ds(0, 12), :] = reduction
        st[x, pl.ds(0, 12), :] = sigma * (zscore * cumulative + density)

        def plane_copy(dx):
            return pltpu.make_async_remote_copy(
                st.at[x], st.at[x], plane_out.at[dx], plane_in.at[x], device_id=(myrow, (x + dx) % 4), device_id_type=MESH
            )

        for dx in range(1, 4):
            plane_copy(dx).start()
        for dx in range(1, 4):
            other = (x + dx) % 4
            pltpu.make_async_remote_copy(
                st.at[other], st.at[other], plane_out.at[dx], plane_in.at[other],
                device_id=(myrow, other), device_id_type=MESH,
            ).wait_recv()
        stat_copy(0, sibling).start()
        for dx in range(1, 4):
            plane_copy(dx).wait_send()
        stat_copy(0, sibling).wait_send()
        drain(slab_out.at[0], NB)

    @pl.when(jnp.logical_not(source))
    def _():
        turned = [(turns + d) % 4 for d in range(4)]
        beside = [pick(turned[d], around) for d in range(4)]
        rows_of = [turned[t] * RC for t in range(4)]

        @pl.when(hub)
        def _():
            best_from_sibling()

        load_cov().wait()
        for p in range(2):
            load_u(p).wait()

        def role_chunk(m, t, lead, d=0):
            part = xs.at[pl.ds(pl.multiple_of(m * KS + (lead * KS + rows_of[t]), RC), RC)]
            return pltpu.make_async_remote_copy(
                part, part, tree_out.at[t, d], chunk_in.at[m * 4 + (lead * 4 + turned[t])],
                device_id=(beside[d], x), device_id_type=MESH,
            )

        def send_on(m, number):
            for t, (_, children) in enumerate(ROLES[number]):
                if children:
                    role_chunk(m, t, EARLY[number]).wait_recv()
                    for d in children:
                        role_chunk(m, t, EARLY[number], d).start()

        def take(m, number):
            for t, (_, children) in enumerate(ROLES[number]):
                if not children:
                    role_chunk(m, t, 0).wait_recv()

        stat_slot = STAT_AT - lookup(node, LEADS)

        def stat_sends(act):
            for d in range(4):
                pl.when(jnp.bitwise_and(lookup(node, FIRST), 1 << d) != 0)(functools.partial(act, d))

        lead = lookup(role, EARLY)

        def forward(m):
            @pl.when(jnp.logical_and(m >= -lead, m < NS - lead))
            def _():
                for number in range(len(ROLES)):
                    pl.when(role == number)(functools.partial(send_on, m, number))

            @pl.when(m >= 0)
            def _():
                for number in range(len(ROLES)):
                    if EARLY[number]:
                        pl.when(role == number)(functools.partial(take, m, number))

            @pl.when(m == stat_slot)
            def _():
                stat_copy(0, sibling).wait_recv()
                stat_sends(lambda d: stat_copy(d, around[d]).start())
                stat_copy(4, sibling).start()

            @pl.when(jnp.logical_and(m == 3 - AHEAD, z == 0))
            def _():
                best_over_z()

        def middle(k, p, j):
            mb[j, pl.ds(pl.multiple_of(p * R, R), R), :] = masked(dot(vt[p], xs[block_rows(k), :]), p)

        def update(j, first, count):
            rows = pl.ds(first, count)
            cols = pl.ds(pl.multiple_of(j * W, W), W)
            res[rows, cols] = (res[rows, cols].astype(F32) - dot(ub[rows, :], mb[j])).astype(BF)

        def block(step, carry):
            k = step - AHEAD // Q
            before = jnp.maximum(k - 1, 0)
            second = before >= NB
            p = second.astype(jnp.int32)
            j = before - NB * p

            def slab(q, carry):
                m = k * Q + q

                @pl.when(hub)
                def _():
                    forward(m)

                    @pl.when(k >= 0)
                    def _():
                        slab_copy(m).start()

                @pl.when(jnp.logical_and(jnp.logical_not(hub), k >= 0))
                def _():
                    slab_copy(m).wait_recv()

                @pl.when(jnp.logical_and(q == 0, k > 0))
                def _():
                    middle(before, p, j)

                for piece in range(2):
                    @pl.when(jnp.logical_and(q == UPDATE_AT[piece], second))
                    def _():
                        update(j, piece * (B // 2), B // 2)

                @pl.when(jnp.logical_and(q == Q - 1, k == 2 * NB - 1))
                def _():
                    acc[...] = dot(vt[1, :, pl.ds(0, B // 2)], xs[block_rows(k, 0, B // 2), :])

                return carry

            return lax.fori_loop(0, Q, slab, carry)

        lax.fori_loop(0, 2 * NB + AHEAD // Q, block, 0)
        rest = dot(vt[1, :, pl.ds(B // 2, B // 2)], xs[block_rows(2 * NB - 1, B // 2, B // 2), :])
        mb[NB - 1, pl.ds(R, R), :] = masked(acc[...] + rest, 1)
        update(NB - 1, 0, B)

        @pl.when(hub)
        def _():
            drain(slab_out.at[0], 2 * NB)
            stat_copy(4, sibling).wait_send()
            stat_sends(lambda d: stat_copy(d, around[d]).wait_send())
            for number, trees in enumerate(ROLES):
                @pl.when(role == number)
                def _():
                    for t, (_, children) in enumerate(trees):
                        for d in children:
                            drain(tree_out.at[t, d], NB // 2)

            @pl.when(jnp.logical_or(z > 0, y > 0))
            def _():
                best_copy(1, 2, sibling).wait_send()

        @pl.when(jnp.logical_not(hub))
        def _():
            stat_copy(0, sibling).wait_recv()

    @pl.when(jnp.logical_not(hub))
    def _():
        best_copy(0, 1, sibling).wait_send()

    stat[...] = st[...]


def place_kernel(res, stat, perm, out, var, imp, lines, slots, sems):
    whole = pltpu.make_async_copy(res, out, sems.at[0])
    whole.start()
    scores = pltpu.make_async_copy(stat, lines, sems.at[1])
    scores.start()
    owners = pltpu.make_async_copy(perm, slots, sems.at[2])
    owners.start()
    var[...] = stat[4, pl.ds(0, 12), :]
    scores.wait()
    owners.wait()

    def pick(i, carry):
        site = slots[i]
        imp[i] = lines[site // B, (site % B) // 128, site % 128]
        return carry

    lax.fori_loop(0, imp.shape[0], pick, 0)
    whole.wait()


def shards(cross_cov, diag_inverse, factor_u, factor_v, rank_ids, weights_obs, observations, prior_var, incumbent, owner_perm):
    hbm = pl.BlockSpec(memory_space=pltpu.HBM)
    vmem = pl.BlockSpec(memory_space=pltpu.VMEM)
    dma = pltpu.SemaphoreType.DMA
    solved, stats = pl.pallas_call(
        solve_kernel,
        name="solve",
        out_shape=(pltpu.VMEM((B, B), BF), pltpu.VMEM((5, 16, 128), F32)),
        in_specs=[hbm] * 9,
        out_specs=(vmem, vmem),
        scratch_shapes=[
            pltpu.VMEM((2 * NB * B, W), BF),
            pltpu.VMEM((B, 2 * R), BF),
            pltpu.VMEM((2, B, R), BF),
            pltpu.VMEM((2, R, B), BF),
            pltpu.VMEM((B, B), BF),
            pltpu.VMEM((NB, 2 * R, W), BF),
            pltpu.VMEM((R, W), F32),
            pltpu.VMEM((24, 128), F32),
            pltpu.VMEM((12, 128), F32),
            pltpu.VMEM((12, 128), F32),
            pltpu.VMEM((5, 16, 128), F32),
            pltpu.VMEM((2, 16, 128), F32),
            pltpu.VMEM((2, 16, 128), F32),
            pltpu.VMEM((8, 8, 128), F32),
            pltpu.SMEM((1, 2), jnp.int32),
            pltpu.SMEM((1,), jnp.int32),
            dma((23,)),
            dma((NS * 4,)),
            dma((NS,)),
            dma((4, 4)),
            dma((1,)),
            dma((8,)),
            dma((3,)),
            dma,
            dma((5,)),
            dma((4,)),
            dma((4,)),
        ],
        compiler_params=pltpu.CompilerParams(collective_id=0, has_side_effects=True, vmem_limit_bytes=48 << 20),
        cost_estimate=pl.CostEstimate(flops=7_250_000_000, bytes_accessed=9_400_000, transcendentals=0),
    )(
        *(
            pltpu.with_memory_space_constraint(array, pltpu.HBM)
            for array in (
                cross_cov, diag_inverse, factor_u, factor_v, rank_ids, weights_obs.reshape(24, 128),
                observations.reshape(12, 128), prior_var.reshape(12, 128),
            )
        ),
        incumbent,
    )
    slots = owner_perm.shape[0]
    result, reduction, improvement = pl.pallas_call(
        place_kernel,
        name="place",
        out_shape=(
            jax.ShapeDtypeStruct((B, B), BF),
            jax.ShapeDtypeStruct((12, 128), F32),
            jax.ShapeDtypeStruct((slots,), F32),
        ),
        in_specs=[vmem, vmem, hbm],
        out_specs=(hbm, vmem, pl.BlockSpec(memory_space=pltpu.SMEM)),
        scratch_shapes=[pltpu.SMEM((5, 16, 128), F32), pltpu.SMEM((slots,), jnp.int32), dma((3,))],
        compiler_params=pltpu.CompilerParams(vmem_limit_bytes=16 << 20),
    )(solved, stats, pltpu.with_memory_space_constraint(owner_perm, pltpu.HBM))
    return result, reduction.reshape(B), improvement


def solution(mesh):
    placed = (
        P("row", "col"), P(), P(None, "row", None), P(None, "row", None), P("row", None),
        P(), P("row"), P("col"), P(), P(("row", "col")),
    )
    return jax.shard_map(
        shards, mesh=mesh, in_specs=placed, out_specs=(P("row", "col"), P("col"), P(("row", "col"))), check_vma=False
    )
```

time: 80.6 us -> 51.5 us (0.64)
  the two profiles are of different devices: /device:TPU:53 before, /device:TPU:52 now
where the time goes in v2:
time: 51.5 us; the launch traced here: 51.3 us
  Pallas kernels  50 us (97%)
  between operations  1.29 us (3%)
    pallas_call x1, Pallas kernels, shards(): pl.pallas_call(solve_kernel, name='solve', out_shape=(pltpu.VMEM((B, B),...  46.9 us
    pallas_call x1, Pallas kernels, shards(): pl.pallas_call(place_kernel, name='place', out_shape=(jax.ShapeDtypeStruc...  3.11 us

profile of v2, /device:TPU:52, one launch (start us, length us, event | category | flops | bytes accessed | tf_op | source)
XLA Modules:
  0.0 51.3 jit_solution(12478671302792699460)
XLA Ops:
  1.3 46.9 %solve.1 = (bf16[1536,1536]{1,0:T(8,128)(2,1)S(1)}, f32[5,16,128]{2,1,0:T(8,128)S(1)}) custom-call(bf16[1536,1536]{1,0:T(8,128)(2,1)} %cov.1, bf16[2,1536,1536]{2,1,0:T(8,128)(2,1)} %dinv.1, bf16[2,1536,384]{2,1,0:T(8,128)(2,1)} %fu.1, bf16[2,1536,384]{2,1,0:T(8,128)(2,1)} %fv.1, s32[1,2]{1,0:T(1,128)} %rank.1, f32[24,128]{1,0:T(8,128)} %bitcast.4, ...), custom_call_target="tpu_custom_call" | custom-call | flops 7249999872 | bytes 9400000 | tf_op jit(solution)/shard_map/solve/pallas_call | solution.py:595
  48.2 3.1 %place.1 = (bf16[1536,1536]{1,0:T(8,128)(2,1)}, f32[12,128]{1,0:T(8,128)}, f32[48]{0:T(128)}) custom-call(bf16[1536,1536]{1,0:T(8,128)(2,1)S(1)} %get-tuple-element.8.res, f32[5,16,128]{2,1,0:T(8,128)S(1)} %get-tuple-element.9.stat, s32[48]{0:T(128)} %perm.1), custom_call_target="tpu_custom_call" | custom-call | tf_op jit(solution)/shard_map/place/pallas_call | solution.py:643

commit v3 on v2

--- a/solution.py
+++ b/solution.py
@@ -11,13 +11,11 @@
 R = 384
 W = 256
 NB = 6
-Q = 2
-KS = B // Q
-RC = KS // 4
-NS = 2 * NB * Q
-AHEAD = 6
+NS = 4 * NB
+HALF = B // 2
+RC = HALF // 4
+AHEAD = 7
 STAT_AT = NS - 1
-UPDATE_AT = {2: (0, 1), 3: (1, 2), 4: (1, 3), 6: (2, 4)}[Q]
 PLACES = (0, 0, 4, 2, 1, 8, 12, 9, 5, 15, 16, 13, 3, 11, 14, 10)
 ROLES = (
     ((1, (0, 1, 3)), (3, ()), (3, ()), (3, ())),
@@ -29,6 +27,7 @@
 EARLY = tuple(AHEAD if any(not children for _, children in role) else 0 for role in ROLES)
 LEADS = tuple(EARLY[place // 4] if ROLES[place // 4][-place % 4][1] else 0 for place in PLACES)
 FIRST = tuple(sum(1 << (d + place) % 4 for d in ROLES[place // 4][-place % 4][1]) for place in PLACES)
+PARTS = 4
 BF = jnp.bfloat16
 F32 = jnp.float32
 
@@ -120,7 +119,7 @@
         return local(dinv.at[(c, *part)], db.at[part], 17 + r)
 
     def load_u(p):
-        return local(fu.at[p], ub.at[:, pl.ds(p * R, R)], 2 + p)
+        return local(fu.at[p], ub.at[p], 2 + p)
 
     def load_v(p):
         return local(fv.at[p], vb.at[p], 4 + p)
@@ -180,29 +179,30 @@
     def block_rows(k, first=0, count=B):
         return pl.ds(pl.multiple_of(k * B + first, 128), count)
 
-    def triangular(k, j):
+    def triangular(k, j, blocks=range(NB)):
         cols = pl.ds(pl.multiple_of(j * W, W), W)
-        for r in range(NB):
+        for r in blocks:
             deep = (r + 1) * W
             xs[block_rows(k, r * W, W), :] = dot(db[pl.ds(r * W, W), pl.ds(0, deep)], res[pl.ds(0, deep), cols]).astype(BF)
-        res[:, cols] = xs[block_rows(k), :]
+        if blocks[-1] == NB - 1:
+            res[:, cols] = xs[block_rows(k), :]
 
     def block_copy(k, place):
         part = xs.at[block_rows(k)]
         return pltpu.make_async_remote_copy(
-            part, part, slab_out.at[place], slab_in.at[k * Q], device_id=(sibling, x), device_id_type=MESH
+            part, part, slab_out.at[place], slab_in.at[k], device_id=(sibling, x), device_id_type=MESH
         )
 
     def slab_copy(m):
-        part = xs.at[pl.ds(pl.multiple_of(m * KS, KS), KS)]
+        part = xs.at[pl.ds(pl.multiple_of(m * HALF, HALF), HALF)]
         return pltpu.make_async_remote_copy(
             part, part, slab_out.at[0], slab_in.at[m], device_id=(sibling, x), device_id_type=MESH
         )
 
-    def chunk_copy(i, t, d):
-        part = xs.at[pl.ds(pl.multiple_of(i * KS + t * RC, RC), RC)]
+    def chunk_copy(i, t):
+        part = xs.at[pl.ds(pl.multiple_of(i * HALF + t * RC, RC), RC)]
         return pltpu.make_async_remote_copy(
-            part, part, tree_out.at[t, d], chunk_in.at[i * 4 + t], device_id=(around[d], x), device_id_type=MESH
+            part, part, tree_out.at[t, t], chunk_in.at[i * 4 + t], device_id=(around[t], x), device_id_type=MESH
         )
 
     def drain(sem, blocks):
@@ -224,12 +224,12 @@
     @pl.when(source)
     def _():
         load_cov_block(0).wait()
-        for r in range(NB):
+        for r in range(NB // 2):
             load_d(r).wait()
 
     @pl.when(myrow == 0)
     def _():
-        triangular(0, 0)
+        triangular(0, 0, range(NB // 2))
 
     @pl.when(myrow > 0)
     def _():
@@ -313,41 +313,47 @@
 
     @pl.when(jnp.logical_and(source, c == 0))
     def _():
-        block_copy(0, 0).start()
-        for j in range(1, NB):
-            load_cov_block(j).wait()
         load_w().wait()
         terms = weights(0)
 
         def slot(s, carry):
-            k = s // Q
-
-            @pl.when(jnp.logical_and(k >= NB, s % Q == 0))
+            k = s // 2
+
+            @pl.when(jnp.logical_and(k >= NB, s % 2 == 0))
             def _():
                 block_copy(k, 0).wait_recv()
 
             for t in range(4):
-                chunk_copy(s, t, t).start()
-
-            @pl.when(jnp.logical_and(s % 2 == 0, s < 10))
-            def _():
-                j = s // 2 + 1
+                chunk_copy(s, t).start()
+
+            @pl.when(s == 0)
+            def _():
+                for r in range(NB // 2, NB):
+                    load_d(r).wait()
+                triangular(0, 0, range(NB // 2, NB))
+                block_copy(0, 0).start()
+                for j in range(1, NB):
+                    load_cov_block(j).wait()
+
+            @pl.when(jnp.logical_and(s % 2 == 1, s < 10))
+            def _():
+                j = (s + 1) // 2
                 triangular(at0(j), j)
                 block_copy(at0(j), 0).start()
 
-            @pl.when(s == 6 * Q)
+            @pl.when(s == 12)
             def _():
                 best_from_sibling()
 
-            @pl.when(s == 6 * Q + 1)
+            @pl.when(s == 13)
             def _():
                 best_over_z()
 
-            @pl.when(s == 7 * Q)
+            @pl.when(s == 14)
             def _():
                 best_over_y()
 
-            after = s - 4 * Q
+            after = s - 8
 
             @pl.when(jnp.logical_and(jnp.logical_and(after >= 0, after < 12), after % 2 == 0))
             def _():
@@ -374,6 +380,8 @@
 
     @pl.when(jnp.logical_and(source, c == 1))
     def _():
+        for r in range(NB // 2, NB):
+            load_d(r).wait()
         for j in range(1, NB):
             load_cov_block(j).wait()
         for p in range(2):
@@ -386,8 +394,8 @@
             first, second = at0(j), at1(j)
             cols = pl.ds(pl.multiple_of(j * W, W), W)
             block_copy(first, 0).wait_recv()
-            mb[0, pl.ds(0, R), :] = masked(dot(vt[0], xs[block_rows(first), :]), 0)
-            res[:, cols] = (res[:, cols].astype(F32) - dot(ub[:, pl.ds(0, R)], mb[0, pl.ds(0, R), :])).astype(BF)
+            mb[...] = masked(dot(vt[0], xs[block_rows(first), :]), 0)
+            res[:, cols] = (res[:, cols].astype(F32) - dot(ub[0], mb[...])).astype(BF)
             triangular(second, j)
             block_copy(second, 0).start()
             tally(second, j, terms)
@@ -440,24 +448,37 @@
         for p in range(2):
             load_u(p).wait()
 
-        def role_chunk(m, t, lead, d=0):
-            part = xs.at[pl.ds(pl.multiple_of(m * KS + (lead * KS + rows_of[t]), RC), RC)]
+        def role_rows(i, t):
+            return xs.at[pl.ds(pl.multiple_of(i * HALF + rows_of[t], RC), RC)]
+
+        def role_chunk(i, t, d=0):
+            part = role_rows(i, t)
             return pltpu.make_async_remote_copy(
-                part, part, tree_out.at[t, d], chunk_in.at[m * 4 + (lead * 4 + turned[t])],
-                device_id=(beside[d], x), device_id_type=MESH,
+                part, part, tree_out.at[t, d], chunk_in.at[i * 4 + turned[t]], device_id=(beside[d], x), device_id_type=MESH
             )
 
-        def send_on(m, number):
+        def send_on(i, number):
             for t, (_, children) in enumerate(ROLES[number]):
                 if children:
-                    role_chunk(m, t, EARLY[number]).wait_recv()
+                    role_chunk(i, t).wait_recv()
                     for d in children:
-                        role_chunk(m, t, EARLY[number], d).start()
-
-        def take(m, number):
+                        role_chunk(i, t, d).start()
+
+        def take(i, number):
             for t, (_, children) in enumerate(ROLES[number]):
                 if not children:
-                    role_chunk(m, t, 0).wait_recv()
+                    role_chunk(i, t).wait_recv()
+
+        def take_last(number):
+            for leaf in (False, True):
+                for t, (_, children) in enumerate(ROLES[number]):
+                    if leaf == (not children):
+                        if leaf:
+                            role_chunk(NS - 1, t).wait_recv()
+                        part = role_rows(NS - 1, t)
+                        pltpu.make_async_remote_copy(
+                            part, part, slab_out.at[0], slab_in.at[NS - 1], device_id=(sibling, x), device_id_type=MESH
+                        ).start()
 
         stat_slot = STAT_AT - lookup(node, LEADS)
 
@@ -468,16 +489,24 @@
         lead = lookup(role, EARLY)
 
         def forward(m):
-            @pl.when(jnp.logical_and(m >= -lead, m < NS - lead))
+            i = m + lead
+
+            @pl.when(jnp.logical_and(i >= 0, i < NS))
             def _():
                 for number in range(len(ROLES)):
-                    pl.when(role == number)(functools.partial(send_on, m, number))
-
-            @pl.when(m >= 0)
+                    pl.when(role == number)(functools.partial(send_on, i, number))
+
+            @pl.when(jnp.logical_and(m >= 0, m < NS - 1))
             def _():
                 for number in range(len(ROLES)):
                     if EARLY[number]:
                         pl.when(role == number)(functools.partial(take, m, number))
+                slab_copy(m).start()
+
+            @pl.when(m == NS - 1)
+            def _():
+                for number in range(len(ROLES)):
+                    pl.when(role == number)(functools.partial(take_last, number))
 
             @pl.when(m == stat_slot)
             def _():
@@ -489,57 +518,49 @@
             def _():
                 best_over_z()
 
-        def middle(k, p, j):
-            mb[j, pl.ds(pl.multiple_of(p * R, R), R), :] = masked(dot(vt[p], xs[block_rows(k), :]), p)
-
-        def update(j, first, count):
+        def middle(k, p):
+            mb[...] = masked(dot(vt[p], xs[block_rows(k), :]), p)
+
+        def update(p, j, first, count):
             rows = pl.ds(first, count)
             cols = pl.ds(pl.multiple_of(j * W, W), W)
-            res[rows, cols] = (res[rows, cols].astype(F32) - dot(ub[rows, :], mb[j])).astype(BF)
-
-        def block(step, carry):
-            k = step - AHEAD // Q
+            res[rows, cols] = (res[rows, cols].astype(F32) - dot(ub[p, rows, :], mb[...])).astype(BF)
+
+        def slot(step, carry):
+            m = step - AHEAD
+            k = jnp.maximum(m, 0) // 2
+            q = jnp.maximum(m, 0) % 2
             before = jnp.maximum(k - 1, 0)
-            second = before >= NB
-            p = second.astype(jnp.int32)
+            p = (before >= NB).astype(jnp.int32)
             j = before - NB * p
 
-            def slab(q, carry):
-                m = k * Q + q
-
-                @pl.when(hub)
+            @pl.when(hub)
+            def _():
+                forward(m)
+
+            @pl.when(jnp.logical_and(jnp.logical_not(hub), m >= 0))
+            def _():
+                slab_copy(m).wait_recv()
+
+            @pl.when(jnp.logical_and(q == 0, jnp.logical_and(k > 0, m > 0)))
+            def _():
+                middle(before, p)
+
+            for piece in range(2):
+                @pl.when(jnp.logical_and(q == piece, k > 0))
                 def _():
-                    forward(m)
-
-                    @pl.when(k >= 0)
-                    def _():
-                        slab_copy(m).start()
-
-                @pl.when(jnp.logical_and(jnp.logical_not(hub), k >= 0))
-                def _():
-                    slab_copy(m).wait_recv()
-
-                @pl.when(jnp.logical_and(q == 0, k > 0))
-                def _():
-                    middle(before, p, j)
-
-                for piece in range(2):
-                    @pl.when(jnp.logical_and(q == UPDATE_AT[piece], second))
-                    def _():
-                        update(j, piece * (B // 2), B // 2)
-
-                @pl.when(jnp.logical_and(q == Q - 1, k == 2 * NB - 1))
-                def _():
-                    acc[...] = dot(vt[1, :, pl.ds(0, B // 2)], xs[block_rows(k, 0, B // 2), :])
-
-                return carry
-
-            return lax.fori_loop(0, Q, slab, carry)
-
-        lax.fori_loop(0, 2 * NB + AHEAD // Q, block, 0)
-        rest = dot(vt[1, :, pl.ds(B // 2, B // 2)], xs[block_rows(2 * NB - 1, B // 2, B // 2), :])
-        mb[NB - 1, pl.ds(R, R), :] = masked(acc[...] + rest, 1)
-        update(NB - 1, 0, B)
+                    update(p, j, piece * HALF, HALF)
+
+            @pl.when(m == NS - 2)
+            def _():
+                acc[...] = dot(vt[1, :, pl.ds(0, B - HALF)], xs[block_rows(2 * NB - 1, 0, B - HALF), :])
+
+            return carry
+
+        lax.fori_loop(0, NS + AHEAD, slot, 0)
+        rest = dot(vt[1, :, pl.ds(B - HALF, HALF)], xs[block_rows(2 * NB - 1, B - HALF, HALF), :])
+        mb[...] = masked(acc[...] + rest, 1)
+        update(1, NB - 1, 0, B)
 
         @pl.when(hub)
         def _():
@@ -569,23 +590,24 @@
 
 
 def place_kernel(res, stat, perm, out, var, imp, lines, slots, sems):
-    whole = pltpu.make_async_copy(res, out, sems.at[0])
-    whole.start()
-    scores = pltpu.make_async_copy(stat, lines, sems.at[1])
+    scores = pltpu.make_async_copy(stat.at[pl.ds(0, 4)], lines, sems.at[PARTS])
     scores.start()
-    owners = pltpu.make_async_copy(perm, slots, sems.at[2])
+    owners = pltpu.make_async_copy(perm, slots, sems.at[PARTS + 1])
     owners.start()
+    step = B // PARTS
+    parts = [pltpu.make_async_copy(res.at[pl.ds(r * step, step)], out.at[pl.ds(r * step, step)], sems.at[r]) for r in range(PARTS)]
+    for part in parts:
+        part.start()
     var[...] = stat[4, pl.ds(0, 12), :]
     scores.wait()
     owners.wait()
-
-    def pick(i, carry):
+    for i in range(imp.shape[0]):
         site = slots[i]
-        imp[i] = lines[site // B, (site % B) // 128, site % 128]
-        return carry
-
-    lax.fori_loop(0, imp.shape[0], pick, 0)
-    whole.wait()
+        line = lax.shift_right_logical(site, 7)
+        plane = lax.shift_right_logical(line * 43, 9)
+        imp[i] = lines[plane, line - 12 * plane, jnp.bitwise_and(site, 127)]
+    for part in parts:
+        part.wait()
 
 
 def shards(cross_cov, diag_inverse, factor_u, factor_v, rank_ids, weights_obs, observations, prior_var, incumbent, owner_perm):
@@ -600,11 +622,11 @@
         out_specs=(vmem, vmem),
         scratch_shapes=[
             pltpu.VMEM((2 * NB * B, W), BF),
-            pltpu.VMEM((B, 2 * R), BF),
+            pltpu.VMEM((2, B, R), BF),
             pltpu.VMEM((2, B, R), BF),
             pltpu.VMEM((2, R, B), BF),
             pltpu.VMEM((B, B), BF),
-            pltpu.VMEM((NB, 2 * R, W), BF),
+            pltpu.VMEM((R, W), BF),
             pltpu.VMEM((R, W), F32),
             pltpu.VMEM((24, 128), F32),
             pltpu.VMEM((12, 128), F32),
@@ -650,7 +672,7 @@
         ),
         in_specs=[vmem, vmem, hbm],
         out_specs=(hbm, vmem, pl.BlockSpec(memory_space=pltpu.SMEM)),
-        scratch_shapes=[pltpu.SMEM((5, 16, 128), F32), pltpu.SMEM((slots,), jnp.int32), dma((3,))],
+        scratch_shapes=[pltpu.SMEM((4, 16, 128), F32), pltpu.SMEM((slots,), jnp.int32), dma((PARTS + 2,))],
         compiler_params=pltpu.CompilerParams(vmem_limit_bytes=16 << 20),
     )(solved, stats, pltpu.with_memory_space_constraint(owner_perm, pltpu.HBM))
     return result, reduction.reshape(B), improvement

time: 51.5 us -> 50.4 us (0.979)
  Pallas kernels: 50 us -> 49 us
    pallas_call x1, Pallas kernels: 46.9 us -> 46.1 us  [shards(): pl.pallas_call(solve_kernel, name='solve', out_shape=(pltpu.VMEM((B, B),...]
where the time goes in v3:
time: 50.4 us; the launch traced here: 50.3 us
  Pallas kernels  49 us (97%)
  between operations  1.29 us (3%)
    pallas_call x1, Pallas kernels, shards(): pl.pallas_call(solve_kernel, name='solve', out_shape=(pltpu.VMEM((B, B),...  46.1 us
    pallas_call x1, Pallas kernels, shards(): pl.pallas_call(place_kernel, name='place', out_shape=(jax.ShapeDtypeStruc...  2.84 us

profile of v3, /device:TPU:52, one launch (start us, length us, event | category | flops | bytes accessed | tf_op | source)
XLA Modules:
  0.0 50.3 jit_solution(5994057195958913583)
XLA Ops:
  1.3 46.1 %solve.1 = (bf16[1536,1536]{1,0:T(8,128)(2,1)S(1)}, f32[5,16,128]{2,1,0:T(8,128)S(1)}) custom-call(bf16[1536,1536]{1,0:T(8,128)(2,1)} %cov.1, bf16[2,1536,1536]{2,1,0:T(8,128)(2,1)} %dinv.1, bf16[2,1536,384]{2,1,0:T(8,128)(2,1)} %fu.1, bf16[2,1536,384]{2,1,0:T(8,128)(2,1)} %fv.1, s32[1,2]{1,0:T(1,128)} %rank.1, f32[24,128]{1,0:T(8,128)} %bitcast.4, ...), custom_call_target="tpu_custom_call" | custom-call | flops 7249999872 | bytes 9400000 | tf_op jit(solution)/shard_map/solve/pallas_call | solution.py:617
  47.4 2.8 %place.1 = (bf16[1536,1536]{1,0:T(8,128)(2,1)}, f32[12,128]{1,0:T(8,128)}, f32[48]{0:T(128)}) custom-call(bf16[1536,1536]{1,0:T(8,128)(2,1)S(1)} %get-tuple-element.8.res, f32[5,16,128]{2,1,0:T(8,128)S(1)} %get-tuple-element.9.stat, s32[48]{0:T(128)} %perm.1), custom_call_target="tpu_custom_call" | custom-call | tf_op jit(solution)/shard_map/place/pallas_call | solution.py:665

commit v4 on v3

--- a/solution.py
+++ b/solution.py
@@ -111,7 +111,7 @@
         return local(cov, res, 0)
 
     def load_cov_block(j):
-        cols = pl.ds(j * W, W)
+        cols = pl.ds(pl.multiple_of(j * W, W), W)
         return local(cov.at[:, cols], res.at[:, cols], 11 + j)
 
     def load_d(r):
@@ -332,12 +332,11 @@
                     load_d(r).wait()
                 triangular(0, 0, range(NB // 2, NB))
                 block_copy(0, 0).start()
-                for j in range(1, NB):
-                    load_cov_block(j).wait()
 
             @pl.when(jnp.logical_and(s % 2 == 1, s < 10))
             def _():
                 j = (s + 1) // 2
+                load_cov_block(j).wait()
                 triangular(at0(j), j)
                 block_copy(at0(j), 0).start()
 
@@ -542,14 +541,13 @@
             def _():
                 slab_copy(m).wait_recv()
 
-            @pl.when(jnp.logical_and(q == 0, jnp.logical_and(k > 0, m > 0)))
-            def _():
-                middle(before, p)
-
-            for piece in range(2):
-                @pl.when(jnp.logical_and(q == piece, k > 0))
-                def _():
-                    update(p, j, piece * HALF, HALF)
+            @pl.when(jnp.logical_and(q == 0, k > 0))
+            def _():
+                update(p, j, 0, B)
+
+            @pl.when(jnp.logical_and(q == 1, k < 2 * NB - 1))
+            def _():
+                middle(k, (k >= NB).astype(jnp.int32))
 
             @pl.when(m == NS - 2)
             def _():

time: 50.4 us -> 49.8 us (0.988)
  Pallas kernels: 49 us -> 48.3 us
    pallas_call x1, Pallas kernels: 46.1 us -> 45.5 us  [shards(): pl.pallas_call(solve_kernel, name='solve', out_shape=(pltpu.VMEM((B, B),...]
where the time goes in v4:
time: 49.8 us; the launch traced here: 49.6 us
  Pallas kernels  48.3 us (97%)
  between operations  1.29 us (3%)
    pallas_call x1, Pallas kernels, shards(): pl.pallas_call(solve_kernel, name='solve', out_shape=(pltpu.VMEM((B, B),...  45.5 us
    pallas_call x1, Pallas kernels, shards(): pl.pallas_call(place_kernel, name='place', out_shape=(jax.ShapeDtypeStruc...  2.84 us

profile of v4, /device:TPU:52, one launch (start us, length us, event | category | flops | bytes accessed | tf_op | source)
XLA Modules:
  0.0 49.6 jit_solution(1439314802286737872)
XLA Ops:
  1.3 45.5 %solve.1 = (bf16[1536,1536]{1,0:T(8,128)(2,1)S(1)}, f32[5,16,128]{2,1,0:T(8,128)S(1)}) custom-call(bf16[1536,1536]{1,0:T(8,128)(2,1)} %cov.1, bf16[2,1536,1536]{2,1,0:T(8,128)(2,1)} %dinv.1, bf16[2,1536,384]{2,1,0:T(8,128)(2,1)} %fu.1, bf16[2,1536,384]{2,1,0:T(8,128)(2,1)} %fv.1, s32[1,2]{1,0:T(1,128)} %rank.1, f32[24,128]{1,0:T(8,128)} %bitcast.4, ...), custom_call_target="tpu_custom_call" | custom-call | flops 7249999872 | bytes 9400000 | tf_op jit(solution)/shard_map/solve/pallas_call | solution.py:615
  46.8 2.8 %place.1 = (bf16[1536,1536]{1,0:T(8,128)(2,1)}, f32[12,128]{1,0:T(8,128)}, f32[48]{0:T(128)}) custom-call(bf16[1536,1536]{1,0:T(8,128)(2,1)S(1)} %get-tuple-element.8.res, f32[5,16,128]{2,1,0:T(8,128)S(1)} %get-tuple-element.9.stat, s32[48]{0:T(128)} %perm.1), custom_call_target="tpu_custom_call" | custom-call | tf_op jit(solution)/shard_map/place/pallas_call | solution.py:663
